TPU v7x, 32 devices: a whole 2x2x4 slice. The times are simulated.
32 devices in a mesh: cuts: 2 (over x), wide: 8 (over z, y), narrow: 2 (over core).
Axes of the slice: x: 2, y: 2, z: 4, core: 2. Of those that a mesh axis runs over, the one named last changes fastest.
Arguments:
- stem_tensor: float32 [2, 16384, 512], P(None, ('cuts', 'wide', 'narrow')), parts along dimension 1, may hold values from -6 to 6
- leaves: bfloat16 [16, 4, 2, 512, 512], P(('cuts', 'wide')), parts along dimension 0, may hold values from -1 to 1
- root_devices: int32 [4], replicated, may hold values from 0 to 7, as said below
- mode_orders: int32 [4, 9], replicated, may hold values from 0 to 8, each once within a row
Outputs:
- contracted: float32 [2, 16384, 512], P(None, ('cuts', 'wide', 'narrow')), parts along dimension 1
There are 2 independent parts, one for each index of `cuts`. A program takes and returns all parts, laid end to end along the dimension named above; an argument that names none is the same for every part. Nothing has to cross between parts.
Inputs may be any that keep to these rules, and one draw needn't show every extreme that they name: `root_devices`: the roots include 0, 4 and 7. `mode_orders`: each row holds every number of 0 to 8 once.
All inputs are finite; a program needn't handle non-finite values.
Results may differ from a plain program's by a relative error of at most 0.0081.
Values may be sent and summed in bfloat16 or wider, within the bound.
No kernel may reach another device: no remote copies, remote signals or barrier semaphores. Data moves between devices by JAX's collectives and lax.ppermute only.
A program may use at most 64 MiB of HBM per device.

v0:
```python
import functools

import jax
import jax.numpy as jnp
from jax import lax
from jax.experimental import pallas as pl
from jax.experimental.pallas import tpu as pltpu
from jax.sharding import PartitionSpec as P

F32, BF16, I32 = jnp.float32, jnp.bfloat16, jnp.int32
NN = (((1,), (0,)), ((), ()))
NT = (((1,), (1,)), ((), ()))
LIMIT = 48 * 1024 * 1024
SEND_LIMIT = 61 * 1024 * 1024
KEEP_LIMIT = 48 * 1024 * 1024
CHUNKS_TWO, CHUNKS_FOUR = 2, 2
CUTS_TWO, CUTS_FOUR = 1, 1


def dot(left, right, dims=NN):
    return lax.dot_general(left, right, dims, preferred_element_type=F32)


def complex_dot(lr, li, rr, ri):
    left = jnp.concatenate([lr, li], 1)
    return (
        dot(left, jnp.concatenate([rr, -ri], 0)),
        dot(left, jnp.concatenate([ri, rr], 0)),
    )


def source_of(column, modes_ref, step, modes, permuted):
    total = jnp.zeros_like(column)
    for b in range(modes):
        weight = jnp.left_shift(jnp.int32(1), modes_ref[step, b])
        total = total + jnp.where((column >> b) & 1 == 1, weight, 0)
    return jnp.where(permuted == 1, total, column)


def place():
    w = lax.axis_index("wide")
    return w & 1, w >> 1 & 1, w >> 2, lax.axis_index("narrow")


def steps_of(plan, roots_ref, y, group):
    if plan is not None:
        low, high = (jnp.int32(k) for k in plan)
    else:
        low = high = None
        for k in range(roots_ref.shape[0]):
            mine = roots_ref[k] >> 2 == group
            high = jnp.where(mine, k, 0 if high is None else high)
        for k in reversed(range(roots_ref.shape[0])):
            mine = roots_ref[k] >> 2 == group
            low = jnp.where(mine, k, k if low is None else low)
    return jnp.where(y == 0, low, high), jnp.where(y == 0, high, low)


def send_kernel(plan, roots_ref, modes_ref, leaves_ref, *refs):
    sends, (leaf_ref, sem) = refs[:-2], refs[-2:]
    part, width = sends[0].shape[1:]
    rows = part * len(sends)
    y, zb, group, core = place()
    _, step = steps_of(plan, roots_ref, y, group)

    @pl.when(y == 0)
    def _():
        copies = []
        for i, send_ref in enumerate(sends):
            at = pl.ds(pl.multiple_of(core * rows + i * part, part), part)
            copies.append(
                pltpu.make_async_copy(leaves_ref.at[0, step, :, at], send_ref, sem.at[i])
            )
            copies[-1].start()
        for copy in copies:
            copy.wait()

    @pl.when(y == 1)
    def _():
        copy = pltpu.make_async_copy(leaves_ref.at[0, step], leaf_ref, sem.at[0])
        copy.start()
        column = lax.broadcasted_iota(I32, (rows, 1), 0) + core * rows
        source = source_of(column, modes_ref, step, modes_ref.shape[1], zb)
        picked = lax.broadcasted_iota(I32, (rows, width), 1) == source
        picked = jnp.where(picked, 1.0, 0.0).astype(BF16)
        copy.wait()
        for p in range(2):
            made = dot(picked, leaf_ref[p], NT).astype(BF16)
            for i, send_ref in enumerate(sends):
                send_ref[p] = made[i * part : (i + 1) * part]


def keep_kernel(plan, roots_ref, modes_ref, leaves_ref, keep_ref, leaf_ref, sem):
    width = keep_ref.shape[2]
    y, zb, group, core = place()
    step, _ = steps_of(plan, roots_ref, y, group)
    copy = pltpu.make_async_copy(leaves_ref.at[0, step], leaf_ref, sem.at[0])
    copy.start()
    copy.wait()

    @pl.when(y == 0)
    def _():
        same = lax.broadcasted_iota(I32, (width, width), 0) == lax.broadcasted_iota(
            I32, (width, width), 1
        )
        same = jnp.where(same, 1.0, 0.0).astype(BF16)
        for p in range(2):
            keep_ref[p] = dot(same, leaf_ref[p], NT).astype(BF16)

    @pl.when(y == 1)
    def _():
        column = lax.broadcasted_iota(I32, (1, width), 1)
        source = source_of(column, modes_ref, step, modes_ref.shape[1], zb)
        picked = lax.broadcasted_iota(I32, (width, width), 0) == source
        picked = jnp.where(picked, 1.0, 0.0).astype(BF16)
        for p in range(2):
            keep_ref[p] = dot(leaf_ref[p], picked).astype(BF16)


def leaf_call(kernel, limit, parts, rows, plan, roots, modes, leaves):
    width = leaves.shape[-1]
    return pl.pallas_call(
        functools.partial(kernel, plan),
        grid_spec=pltpu.PrefetchScalarGridSpec(
            num_scalar_prefetch=2,
            grid=(1,),
            in_specs=[pl.BlockSpec(memory_space=pl.ANY)],
            out_specs=[whole((2, rows, width))] * parts,
            scratch_shapes=[pltpu.VMEM((2, width, width), BF16), pltpu.SemaphoreType.DMA((parts,))],
        ),
        out_shape=[jax.ShapeDtypeStruct((2, rows, width), BF16)] * parts,
        compiler_params=pltpu.CompilerParams(vmem_limit_bytes=limit),
    )(roots, modes, leaves)


def whole(shape):
    return pl.BlockSpec(shape, lambda i, *_: (0,) * len(shape))


def call(kernel, arrays, outs):
    return pl.pallas_call(
        kernel,
        grid=(1,),
        in_specs=[whole(a.shape) for a in arrays],
        out_specs=[whole(o.shape) for o in outs],
        out_shape=outs,
        compiler_params=pltpu.CompilerParams(vmem_limit_bytes=LIMIT),
    )(*arrays)


def pair_kernel(left_ref, right_ref, out_ref):
    re, im = complex_dot(left_ref[0], left_ref[1], right_ref[0], right_ref[1])
    out_ref[0] = re.astype(BF16)
    out_ref[1] = im.astype(BF16)


def branch_kernel(chunks, cuts, *refs):
    own, got, own_sib, got_sib = (refs[i * chunks : (i + 1) * chunks] for i in range(4))
    firsts, other_ref = refs[4 * chunks : 4 * chunks + cuts], refs[4 * chunks + cuts]
    y, zb, _, core = place()
    rows, width = own[0].shape[1] * chunks, own[0].shape[2]
    part = rows // 2
    high_here = y == zb

    def joined(group, p, at=slice(None)):
        values = [ref[p, :, at] for ref in group]
        return values[0] if len(values) == 1 else jnp.concatenate(values, 0)

    def multiply(left, near, far):
        re = im = None
        for side, right in ((core, near), (1 - core, far)):
            at = pl.ds(pl.multiple_of(side * rows, rows), rows)
            r, m = complex_dot(
                joined(left, 0, at), joined(left, 1, at), joined(right, 0), joined(right, 1)
            )
            re, im = (r, m) if re is None else (re + r, im + m)
        return re.astype(BF16), im.astype(BF16)

    def store(p, top, bottom):
        for here, first, second in ((0, top, bottom), (1, bottom, top)):

            @pl.when(zb == here)
            def _():
                for i, ref in enumerate(firsts):
                    ref[p] = first[i * part // cuts : (i + 1) * part // cuts]
                if len(other_ref.shape) == 4:
                    other_ref[0, p] = first
                    other_ref[1, p] = second
                else:
                    other_ref[p] = second

    def finish(parts):
        @pl.when(y == 1)
        def _():
            for p, value in enumerate(parts):
                store(p, value[:part], value[part:])

        @pl.when(y == 0)
        def _():
            same = lax.broadcasted_iota(I32, (rows, rows), 0) == lax.broadcasted_iota(
                I32, (rows, rows), 1
            )
            same = jnp.where(same, 1.0, 0.0).astype(BF16)
            for p, value in enumerate(parts):
                turned = [dot(same, value[:, i : i + rows], NT) for i in range(0, width, rows)]
                both = jnp.concatenate(turned, 1).astype(BF16)
                store(p, both[:part], both[part:])

    @pl.when(high_here)
    def _():
        finish(multiply(got, own, own_sib))

    @pl.when(jnp.logical_not(high_here))
    def _():
        finish(multiply(own, got, got_sib))


def stem_kernel(plans, turn, layout, roots_ref, own_hbm, sib_hbm, *refs):
    pieces, (out_hbm, o_ref, n1_ref, own_ref, sib_ref, out_ref, sem) = refs[:-7], refs[-7:]
    items = 4
    y, zb, group, core = place()
    zb = zb if turn else 0
    width = own_hbm.shape[2]
    half = width // 2
    part = half // 2
    first = [
        pltpu.make_async_copy(own_hbm, own_ref, sem.at[items]),
        pltpu.make_async_copy(sib_hbm, sib_ref, sem.at[items + 1]),
    ]
    for copy in first:
        copy.start()
    for m in range(items):
        plan = plans[m // 2] if plans else None
        steps = steps_of(plan, roots_ref, y, group if m < 2 else 1 - group)
        step = steps[m % 2]
        column = y if m % 2 == 0 else 1 - y
        for ref, (item, far, halves) in zip(pieces, layout):
            if item != m:
                continue
            side = 1 - core if far else core
            for h, offset in halves:
                source = ref if len(halves) == 1 else ref.at[h]
                count = source.shape[1]
                for s in range(2):
                    row = jnp.where(column == 1, side, s) * half + offset
                    row = row + (1 - zb if h else zb) * part
                    col = jnp.where(column == 1, s, side) * half
                    pltpu.make_async_copy(
                        source.at[:, :, s * half : (s + 1) * half],
                        o_ref.at[
                            step,
                            :,
                            pl.ds(pl.multiple_of(row, count), count),
                            pl.ds(pl.multiple_of(col, half), half),
                        ],
                        sem.at[step],
                    ).start()

    def arrived(step):
        pltpu.make_async_copy(o_ref.at[step], o_ref.at[step], sem.at[step]).wait()

    for copy in first:
        copy.wait()
    arrived(0)
    for f, ref in ((core, own_ref), (1 - core, sib_ref)):
        at = pl.ds(pl.multiple_of(f * half, half), half)
        t = complex_dot(ref[0], ref[1], o_ref[0, 0], o_ref[0, 1])
        for p in range(2):
            value = t[p].astype(BF16)
            for e in range(2):
                n1_ref[e, p, :, at] = value[:, e * half : (e + 1) * half]
    mine = pl.ds(pl.multiple_of(core * half, half), half)
    arrived(1)
    arrived(2)
    o12 = complex_dot(o_ref[1, 0], o_ref[1, 1], o_ref[2, 0, :, mine], o_ref[2, 1, :, mine])
    o12 = [v.astype(BF16) for v in o12]
    arrived(3)
    rows = own_ref.shape[1]
    copies = []
    for r in range(2):
        band = slice(r * rows // 2, (r + 1) * rows // 2)
        n4 = [complex_dot(n1_ref[e, 0, band], n1_ref[e, 1, band], *o12) for e in range(2)]
        n4 = [jnp.concatenate([n4[0][p], n4[1][p]], 1).astype(BF16) for p in range(2)]
        made = complex_dot(*n4, o_ref[3, 0], o_ref[3, 1])
        for p in range(2):
            out_ref[p, band] = made[p]
        copy = pltpu.make_async_copy(
            out_ref.at[:, band], out_hbm.at[:, band], sem.at[items + 2 + r]
        )
        copy.start()
        copies.append(copy)
    for copy in copies:
        copy.wait()


def stem_call(plans, turn, roots, own, sib, items):
    shape = own.shape
    width = shape[2]
    pieces, layout = [], []
    for m, item in enumerate(items):
        for array, far, halves in item:
            pieces.append(array)
            layout.append((m, far, halves))
    anywhere = pl.BlockSpec(memory_space=pl.ANY)
    return pl.pallas_call(
        functools.partial(stem_kernel, plans, turn, tuple(layout)),
        grid_spec=pltpu.PrefetchScalarGridSpec(
            num_scalar_prefetch=1,
            grid=(1,),
            in_specs=[anywhere] * (2 + len(pieces)),
            out_specs=anywhere,
            scratch_shapes=[
                pltpu.VMEM((len(items), 2, width, width), BF16),
                pltpu.VMEM((2, *shape), BF16),
                pltpu.VMEM(shape, BF16),
                pltpu.VMEM(shape, BF16),
                pltpu.VMEM(shape, F32),
                pltpu.SemaphoreType.DMA((len(items) + 4,)),
            ],
        ),
        out_shape=jax.ShapeDtypeStruct(shape, F32),
        compiler_params=pltpu.CompilerParams(vmem_limit_bytes=LIMIT),
    )(roots, own, sib, *pieces)


def swap(value, axis, bit):
    n = lax.axis_size(axis)
    return lax.ppermute(value, axis, [(i, i ^ bit) for i in range(n)])


def other_core(value):
    return swap(value, "narrow", 1)


def select_kernel(plan, roots_ref, made_ref, other_ref, out_ref):
    y, _, group, _ = place()
    step, _ = steps_of(plan, roots_ref, y, group)
    owned = roots_ref[step] >> 2 == group

    @pl.when(owned)
    def _():
        out_ref[...] = made_ref[...]

    @pl.when(jnp.logical_not(owned))
    def _():
        out_ref[...] = other_ref[...]


def select_call(plan, roots, made, other):
    return pl.pallas_call(
        functools.partial(select_kernel, plan),
        grid_spec=pltpu.PrefetchScalarGridSpec(
            num_scalar_prefetch=1,
            grid=(1,),
            in_specs=[whole(made.shape)] * 2,
            out_specs=whole(made.shape),
        ),
        out_shape=jax.ShapeDtypeStruct(made.shape, made.dtype),
        compiler_params=pltpu.CompilerParams(vmem_limit_bytes=LIMIT),
    )(roots, made, other)


def after(value, other):
    return lax.optimization_barrier((value, other))[0]


def sends_of(leaves, roots, modes, plan, chunks):
    rows = leaves.shape[-1] // lax.axis_size("narrow")
    return leaf_call(send_kernel, SEND_LIMIT, chunks, rows // chunks, plan, roots, modes, leaves)


def tree(leaves, roots, modes, plan, sends, joint, cuts, ahead=None, sent=None):
    width = leaves.shape[-1]
    rows = width // lax.axis_size("narrow")
    chunks = len(sends)
    if sent is not None:
        leaves = after(leaves, sent)
    [keep] = leaf_call(keep_kernel, KEEP_LIMIT, 1, width, plan, roots, modes, leaves)
    lefts = [swap(send, "wide", 1) for send in sends]
    pairs = [
        call(pair_kernel, [left, keep], [jax.ShapeDtypeStruct(left.shape, BF16)])[0]
        for left in lefts
    ]
    gots = [swap(pair, "wide", 2) for pair in pairs]
    held = gots if ahead is None else [after(got, ahead) for got in gots]
    sibs = [other_core(v) for v in pairs + held]
    piece = jax.ShapeDtypeStruct((2, rows // 2, width), BF16)
    cut = jax.ShapeDtypeStruct((2, rows // 2 // cuts, width), BF16)
    other = jax.ShapeDtypeStruct((2, *piece.shape), BF16) if joint else piece
    made = call(
        functools.partial(branch_kernel, chunks, cuts), pairs + gots + sibs, [cut] * cuts + [other]
    )
    return made[:-1], made[-1]


def item_of(firsts, seconds):
    item = []
    for half, group in enumerate((firsts, seconds)):
        for i, piece in enumerate(group):
            place_of = ((half, i * piece.shape[1]),)
            item += [(piece, False, place_of), (other_core(piece), True, place_of)]
    return item


def joint_item(both):
    place_of = ((0, 0), (1, 0))
    return [(both, False, place_of), (other_core(both), True, place_of)]


def all_swapped(values, bit):
    return [swap(value, "wide", bit) for value in values]


def each_own_two(stem, leaves, roots, modes):
    own = stem.astype(BF16)
    sib = other_core(own)
    firsts, both = tree(
        leaves, roots, modes, None, sends_of(leaves, roots, modes, None, CHUNKS_TWO), True, CUTS_TWO
    )
    far = all_swapped(firsts, 4)
    near = [joint_item(both), joint_item(swap(both, "wide", 1))]
    far_second = all_swapped(far, 2)
    away = [item_of(far, far_second), item_of(all_swapped(far, 1), all_swapped(far, 3))]
    return stem_call(None, True, roots, own, sib, near + away)


def any_owners(stem, leaves, roots, modes):
    y, zb, group, _ = place()
    own = stem.astype(BF16)
    sib = other_core(own)
    two = lax.axis_size("wide") == 8
    items, plans, ahead = [], [], None
    every = [(k, k + 1) for k in range(0, leaves.shape[1], 2)]
    sends = [sends_of(leaves, roots, modes, plan, CHUNKS_FOUR) for plan in every]
    for j, plan in enumerate(every):
        firsts, second = tree(
            leaves,
            roots,
            modes,
            plan,
            sends[j],
            False,
            CUTS_FOUR if two else 1,
            ahead,
            sends[1][0] if j == 0 else None,
        )
        owned = roots[2 * j + y] // 4 == group
        if two:
            crossed = all_swapped(firsts, 4)
            ahead = crossed[0]
            here = [select_call(plan, roots, v, c) for v, c in zip(firsts, crossed)]
            seconds = all_swapped(here, 2)
            cross = [all_swapped(here, 1), all_swapped(here, 3)]
        else:
            sums = [
                lax.psum(
                    jnp.where(owned & (zb == 0) & (y == side), v, jnp.zeros_like(v)), "wide"
                )
                for side in range(2)
                for v in (firsts[0], second)
            ]
            here, seconds = ([jnp.where(y == 0, a, b)] for a, b in zip(sums[:2], sums[2:]))
            cross = [[jnp.where(y == 0, b, a)] for a, b in zip(sums[:2], sums[2:])]
        items += [item_of(here, seconds), item_of(*cross)]
        plans.append(plan)
    return stem_call(tuple(plans), two, roots, own, sib, items)


MODE = "cond"


def local(stem_tensor, leaves, root_devices, mode_orders):
    given = (stem_tensor, leaves, root_devices, mode_orders)
    if lax.axis_size("wide") != 8 or MODE == "four":
        return any_owners(*given)
    if MODE == "two":
        return each_own_two(*given)
    return lax.cond(jnp.sum(root_devices // 4) == 2, each_own_two, any_owners, *given)


def solution(mesh):
    placed = (
        P(None, ("cuts", "wide", "narrow"), None),
        P(("cuts", "wide"), None, None, None, None),
        P(),
        P(),
    )
    return jax.shard_map(
        local,
        mesh=mesh,
        in_specs=placed,
        out_specs=P(None, ("cuts", "wide", "narrow"), None),
        check_vma=False,
    )
```

profile of v0, /device:TPU:0, one launch (start us, length us, event | category | flops | bytes accessed | tf_op | source)
XLA Modules:
  0.0 71.8 jit_solution(13320589406023723153)
XLA Ops:
  0.0 1.3 %fusion = s32[]{:T(128)} fusion(s32[4]{0:T(128)} %param.8), kind=kLoop, calls=%fused_computation.4 | loop fusion | flops 63 | bytes 20 | tf_op jit(solution)/shard_map/reduce_sum | solution.py:478
  2.0 68.5 %conditional.1 = (f32[2,512,512]{2,1,0:T(8,128)S(1)}) conditional(s32[]{:T(128)} %convert_element_type.9, (f32[2,512,512]{2,1,0:T(8,128)}, s32[4]{0:T(128)}, s32[4,9]{1,0:T(4,128)}, bf16[1,4,2,512,512]{4,3,2,1,0:T(8,128)(2,1)}) %tuple.14, (f32[2,512,512]{2,1,0:T(8,128)}, s32[4]{0:T(128)}, s32[4,9]{1,0:T(4,128)}, ...), branch_computations={%region_1.2_spmd, %region_2.3_spmd} | conditional | flops 524288 | bytes 72353904 | solution.py:478
  2.2 2.7 %branch_1_fun.6 = (bf16[2,128,512]{2,1,0:T(8,128)(2,1)}, bf16[2,128,512]{2,1,0:T(8,128)(2,1)}) custom-call(s32[4]{0:T(128)} %get-tuple-element.37.roots_ref, s32[4,9]{1,0:T(4,128)} %get-tuple-element.39.modes_ref, bf16[1,4,2,512,512]{4,3,2,1,0:T(8,128)(2,1)} %get-tuple-element.40.leaves_ref), custom_call_target="tpu_custom_call" | custom-call | tf_op jit(solution)/shard_map/cond/branch_1_fun/pallas_call | solution.py:122
  4.9 3.7 %collective-permute-start.34 = (bf16[2,128,512]{2,1,0:T(8,128)(2,1)}, bf16[2,128,512]{2,1,0:T(8,128)(2,1)S(1)}, u32[]{:S(2)}, u32[]{:S(2)}) collective-permute-start(bf16[2,128,512]{2,1,0:T(8,128)(2,1)} %get-tuple-element.41), channel_id=1, source_target_pairs={{0,2},{2,0},{4,6},{6,4},{8,10},{10,8},{12,14},{14,12},{1,3},{3,1},... | collective-permute-start | bytes 786440 | tf_op jit(solution)/shard_map/cond/branch_1_fun/ppermute | solution.py:328
  8.7 2.6 %branch_1_fun.7.right_ref = bf16[2,512,512]{2,1,0:T(8,128)(2,1)S(1)} custom-call(s32[4]{0:T(128)S(1)} %copy-done.9, s32[4,9]{1,0:T(4,128)S(1)} %copy-done.7, bf16[1,4,2,512,512]{4,3,2,1,0:T(8,128)(2,1)} %get-tuple-element.40.leaves_ref), custom_call_target="tpu_custom_call" | custom-call | tf_op jit(solution)/shard_map/cond/branch_1_fun/pallas_call | solution.py:122
  11.3 4.7 %collective-permute-done.34.left_ref = bf16[2,128,512]{2,1,0:T(8,128)(2,1)S(1)} collective-permute-done((bf16[2,128,512]{2,1,0:T(8,128)(2,1)}, bf16[2,128,512]{2,1,0:T(8,128)(2,1)S(1)}, u32[]{:S(2)}, u32[]{:S(2)}) %collective-permute-start.34) | collective-permute-done | bytes 262176 | tf_op jit(solution)/shard_map/cond/branch_1_fun/ppermute | solution.py:328
  16.4 1.6 %collective-permute-start.36 = (bf16[2,128,512]{2,1,0:T(8,128)(2,1)S(1)}, bf16[2,128,512]{2,1,0:T(8,128)(2,1)S(1)}, u32[]{:S(2)}, u32[]{:S(2)}) collective-permute-start(bf16[2,128,512]{2,1,0:T(8,128)(2,1)S(1)} %branch_1_fun.8.refs_0_), channel_id=1, source_target_pairs={{0,4},{2,6},{4,0},{6,2},{8,12},{10,14},{12,8},{14,10},{1,5},{3,7},... | collective-permute-start | bytes 786440 | tf_op jit(solution)/shard_map/cond/branch_1_fun/ppermute | solution.py:328
  18.1 2.7 %collective-permute-done.35.left_ref = bf16[2,128,512]{2,1,0:T(8,128)(2,1)S(1)} collective-permute-done((bf16[2,128,512]{2,1,0:T(8,128)(2,1)}, bf16[2,128,512]{2,1,0:T(8,128)(2,1)S(1)}, u32[]{:S(2)}, u32[]{:S(2)}) %collective-permute-start.35) | collective-permute-done | bytes 262176 | tf_op jit(solution)/shard_map/cond/branch_1_fun/ppermute | solution.py:328
  21.2 1.7 %collective-permute-start.37 = (bf16[2,128,512]{2,1,0:T(8,128)(2,1)S(1)}, bf16[2,128,512]{2,1,0:T(8,128)(2,1)S(1)}, u32[]{:S(2)}, u32[]{:S(2)}) collective-permute-start(bf16[2,128,512]{2,1,0:T(8,128)(2,1)S(1)} %branch_1_fun.9.refs_1_), channel_id=1, source_target_pairs={{0,4},{2,6},{4,0},{6,2},{8,12},{10,14},{12,8},{14,10},{1,5},{3,7},... | collective-permute-start | bytes 786440 | tf_op jit(solution)/shard_map/cond/branch_1_fun/ppermute | solution.py:328
  24.1 4.7 %collective-permute-done.37.refs_3_ = bf16[2,128,512]{2,1,0:T(8,128)(2,1)S(1)} collective-permute-done((bf16[2,128,512]{2,1,0:T(8,128)(2,1)S(1)}, bf16[2,128,512]{2,1,0:T(8,128)(2,1)S(1)}, u32[]{:S(2)}, u32[]{:S(2)}) %collective-permute-start.37) | collective-permute-done | bytes 262176 | tf_op jit(solution)/shard_map/cond/branch_1_fun/ppermute | solution.py:328
  28.8 1.5 %collective-permute-done.41.refs_7_ = bf16[2,128,512]{2,1,0:T(8,128)(2,1)S(1)} collective-permute-done((bf16[2,128,512]{2,1,0:T(8,128)(2,1)S(1)}, bf16[2,128,512]{2,1,0:T(8,128)(2,1)S(1)}, u32[]{:S(2)}, u32[]{:S(2)}) %collective-permute-start.41) | collective-permute-done | bytes 262176 | tf_op jit(solution)/shard_map/cond/branch_1_fun/ppermute | solution.py:328
  30.3 1.3 %branch_1_fun.10 = (bf16[2,128,512]{2,1,0:T(8,128)(2,1)S(1)}, bf16[2,2,128,512]{3,2,1,0:T(8,128)(2,1)S(1)}) custom-call(bf16[2,128,512]{2,1,0:T(8,128)(2,1)S(1)} %branch_1_fun.8.refs_0_, bf16[2,128,512]{2,1,0:T(8,128)(2,1)S(1)} %branch_1_fun.9.refs_1_, bf16[2,128,512]{2,1,0:T(8,128)(2,1)S(1)} %collective-permute-done.36.refs_2_, ...), custom_call_target="tpu_custom_call" | custom-call | tf_op jit(solution)/shard_map/cond/branch_1_fun/pallas_call | solution.py:141
  31.6 2.7 %collective-permute-start.45 = (bf16[2,128,512]{2,1,0:T(8,128)(2,1)S(1)}, bf16[2,128,512]{2,1,0:T(8,128)(2,1)S(1)}, u32[]{:S(2)}, u32[]{:S(2)}) collective-permute-start(bf16[2,128,512]{2,1,0:T(8,128)(2,1)S(1)} %get-tuple-element.44), channel_id=1, source_target_pairs={{0,8},{2,10},{4,12},{6,14},{8,0},{10,2},{12,4},{14,6},{1,9},{3,11}... | collective-permute-start | bytes 786440 | tf_op jit(solution)/shard_map/cond/branch_1_fun/ppermute | solution.py:328
  34.3 1.2 %collective-permute-start.43 = (bf16[2,2,128,512]{3,2,1,0:T(8,128)(2,1)S(1)}, bf16[2,2,128,512]{3,2,1,0:T(8,128)(2,1)S(1)}, u32[]{:S(2)}, u32[]{:S(2)}) collective-permute-start(bf16[2,2,128,512]{3,2,1,0:T(8,128)(2,1)S(1)} %get-tuple-element.43.refs_0_), channel_id=1, source_target_pairs={{0,2},{2,0},{4,6},{6,4},{8,10},{10,8},{12,14},{14,12},{1,3},{3,1},... | collective-permute-start | bytes 1572872 | tf_op jit(solution)/shard_map/cond/branch_1_fun/ppermute | solution.py:328
  35.5 11.0 %collective-permute-done.45.refs_4_ = bf16[2,128,512]{2,1,0:T(8,128)(2,1)S(1)} collective-permute-done((bf16[2,128,512]{2,1,0:T(8,128)(2,1)S(1)}, bf16[2,128,512]{2,1,0:T(8,128)(2,1)S(1)}, u32[]{:S(2)}, u32[]{:S(2)}) %collective-permute-start.45) | collective-permute-done | bytes 262176 | tf_op jit(solution)/shard_map/cond/branch_1_fun/ppermute | solution.py:328
  46.5 1.4 %collective-permute-start.51 = (bf16[2,128,512]{2,1,0:T(8,128)(2,1)S(1)}, bf16[2,128,512]{2,1,0:T(8,128)(2,1)S(1)}, u32[]{:S(2)}, u32[]{:S(2)}) collective-permute-start(bf16[2,128,512]{2,1,0:T(8,128)(2,1)S(1)} %collective-permute-done.45.refs_4_), channel_id=1, source_target_pairs={{0,6},{2,4},{4,2},{6,0},{8,14},{10,12},{12,10},{14,8},{1,7},{3,5},... | collective-permute-start | bytes 786440 | tf_op jit(solution)/shard_map/cond/branch_1_fun/ppermute | solution.py:328
  47.9 0.8 %collective-permute-start.49 = (bf16[2,128,512]{2,1,0:T(8,128)(2,1)S(1)}, bf16[2,128,512]{2,1,0:T(8,128)(2,1)S(1)}, u32[]{:S(2)}, u32[]{:S(2)}) collective-permute-start(bf16[2,128,512]{2,1,0:T(8,128)(2,1)S(1)} %collective-permute-done.45.refs_4_), channel_id=1, source_target_pairs={{0,2},{2,0},{4,6},{6,4},{8,10},{10,8},{12,14},{14,12},{1,3},{3,1},... | collective-permute-start | bytes 786440 | tf_op jit(solution)/shard_map/cond/branch_1_fun/ppermute | solution.py:328
  48.7 1.3 %collective-permute-start.47 = (bf16[2,128,512]{2,1,0:T(8,128)(2,1)S(1)}, bf16[2,128,512]{2,1,0:T(8,128)(2,1)S(1)}, u32[]{:S(2)}, u32[]{:S(2)}) collective-permute-start(bf16[2,128,512]{2,1,0:T(8,128)(2,1)S(1)} %collective-permute-done.45.refs_4_), channel_id=1, source_target_pairs={{0,4},{2,6},{4,0},{6,2},{8,12},{10,14},{12,8},{14,10},{1,5},{3,7},... | collective-permute-start | bytes 786440 | tf_op jit(solution)/shard_map/cond/branch_1_fun/ppermute | solution.py:328
  50.0 6.7 %collective-permute-done.51.refs_10_ = bf16[2,128,512]{2,1,0:T(8,128)(2,1)S(1)} collective-permute-done((bf16[2,128,512]{2,1,0:T(8,128)(2,1)S(1)}, bf16[2,128,512]{2,1,0:T(8,128)(2,1)S(1)}, u32[]{:S(2)}, u32[]{:S(2)}) %collective-permute-start.51) | collective-permute-done | bytes 262176 | tf_op jit(solution)/shard_map/cond/branch_1_fun/ppermute | solution.py:328
  56.7 0.5 collective-permute-start.44
  57.2 3.3 %collective-permute-done.49.refs_8_ = bf16[2,128,512]{2,1,0:T(8,128)(2,1)S(1)} collective-permute-done((bf16[2,128,512]{2,1,0:T(8,128)(2,1)S(1)}, bf16[2,128,512]{2,1,0:T(8,128)(2,1)S(1)}, u32[]{:S(2)}, u32[]{:S(2)}) %collective-permute-start.49) | collective-permute-done | bytes 262176 | tf_op jit(solution)/shard_map/cond/branch_1_fun/ppermute | solution.py:328
  61.1 0.9 %collective-permute-done.52.refs_11_ = bf16[2,128,512]{2,1,0:T(8,128)(2,1)S(1)} collective-permute-done((bf16[2,128,512]{2,1,0:T(8,128)(2,1)S(1)}, bf16[2,128,512]{2,1,0:T(8,128)(2,1)S(1)}, u32[]{:S(2)}, u32[]{:S(2)}) %collective-permute-start.52) | collective-permute-done | bytes 262176 | tf_op jit(solution)/shard_map/cond/branch_1_fun/ppermute | solution.py:328
  62.8 7.6 %branch_1_fun.11 = f32[2,512,512]{2,1,0:T(8,128)S(1)} custom-call(s32[4]{0:T(128)S(1)} %copy-done.9, bf16[2,512,512]{2,1,0:T(8,128)(2,1)S(1)} %convert_element_type.7.own_hbm, bf16[2,512,512]{2,1,0:T(8,128)(2,1)} %copy-done.5, bf16[2,2,128,512]{3,2,1,0:T(8,128)(2,1)S(1)} %get-tuple-element.43.refs_0_, ...), custom_call_target="tpu_custom_call" | custom-call | tf_op jit(solution)/shard_map/cond/branch_1_fun/pallas_call | solution.py:305
  70.5 1.3 %copy-done.3 = f32[2,512,512]{2,1,0:T(8,128)} copy-done((f32[2,512,512]{2,1,0:T(8,128)}, f32[2,512,512]{2,1,0:T(8,128)S(1)}, u32[]{:S(2)}) %copy-start.3) | copy-done | bytes 2097176
  (35 shorter events, 3.6 us)
Async XLA Ops:
  2.2 6.5 %copy-start.7 = (s32[4,9]{1,0:T(4,128)S(1)}, s32[4,9]{1,0:T(4,128)}, u32[]{:S(2)}) copy-start(s32[4,9]{1,0:T(4,128)} %get-tuple-element.39.modes_ref) | copy-start | bytes 436 | tf_op jit(solution)/shard_map/cond
  2.2 6.5 %copy-start.9 = (s32[4]{0:T(128)S(1)}, s32[4]{0:T(128)}, u32[]{:S(2)}) copy-start(s32[4]{0:T(128)} %get-tuple-element.37.roots_ref) | copy-start | bytes 52 | tf_op jit(solution)/shard_map/cond
  4.9 11.1 %collective-permute-start.34 = (bf16[2,128,512]{2,1,0:T(8,128)(2,1)}, bf16[2,128,512]{2,1,0:T(8,128)(2,1)S(1)}, u32[]{:S(2)}, u32[]{:S(2)}) collective-permute-start(bf16[2,128,512]{2,1,0:T(8,128)(2,1)} %get-tuple-element.41), channel_id=1, source_target_pairs={{0,2},{2,0},{4,6},{6,4},{8,10},{10,8},{12,14},{14,12},{1,3},{3,1},... | collective-permute-start | bytes 786440 | tf_op jit(solution)/shard_map/cond/branch_1_fun/ppermute | solution.py:328
  8.6 12.1 %collective-permute-start.35 = (bf16[2,128,512]{2,1,0:T(8,128)(2,1)}, bf16[2,128,512]{2,1,0:T(8,128)(2,1)S(1)}, u32[]{:S(2)}, u32[]{:S(2)}) collective-permute-start(bf16[2,128,512]{2,1,0:T(8,128)(2,1)} %get-tuple-element.42), channel_id=1, source_target_pairs={{0,2},{2,0},{4,6},{6,4},{8,10},{10,8},{12,14},{14,12},{1,3},{3,1},... | collective-permute-start | bytes 786440 | tf_op jit(solution)/shard_map/cond/branch_1_fun/ppermute | solution.py:328
  11.3 11.6 %copy-start.2 = (f32[2,512,512]{2,1,0:T(8,128)S(1)}, f32[2,512,512]{2,1,0:T(8,128)}, u32[]{:S(2)}) copy-start(f32[2,512,512]{2,1,0:T(8,128)} %get-tuple-element.38) | copy-start | bytes 6291460 | tf_op jit(solution)/shard_map/cond
  16.4 7.2 %collective-permute-start.36 = (bf16[2,128,512]{2,1,0:T(8,128)(2,1)S(1)}, bf16[2,128,512]{2,1,0:T(8,128)(2,1)S(1)}, u32[]{:S(2)}, u32[]{:S(2)}) collective-permute-start(bf16[2,128,512]{2,1,0:T(8,128)(2,1)S(1)} %branch_1_fun.8.refs_0_), channel_id=1, source_target_pairs={{0,4},{2,6},{4,0},{6,2},{8,12},{10,14},{12,8},{14,10},{1,5},{3,7},... | collective-permute-start | bytes 786440 | tf_op jit(solution)/shard_map/cond/branch_1_fun/ppermute | solution.py:328
  21.2 7.6 %collective-permute-start.37 = (bf16[2,128,512]{2,1,0:T(8,128)(2,1)S(1)}, bf16[2,128,512]{2,1,0:T(8,128)(2,1)S(1)}, u32[]{:S(2)}, u32[]{:S(2)}) collective-permute-start(bf16[2,128,512]{2,1,0:T(8,128)(2,1)S(1)} %branch_1_fun.9.refs_1_), channel_id=1, source_target_pairs={{0,4},{2,6},{4,0},{6,2},{8,12},{10,14},{12,8},{14,10},{1,5},{3,7},... | collective-permute-start | bytes 786440 | tf_op jit(solution)/shard_map/cond/branch_1_fun/ppermute | solution.py:328
  23.0 25.7 %collective-permute-start.33 = (bf16[2,512,512]{2,1,0:T(8,128)(2,1)S(1)}, bf16[2,512,512]{2,1,0:T(8,128)(2,1)S(1)}, u32[]{:S(2)}, u32[]{:S(2)}) collective-permute-start(bf16[2,512,512]{2,1,0:T(8,128)(2,1)S(1)} %convert_element_type.7.own_hbm), channel_id=1, source_target_pairs={{0,1},{1,0},{2,3},{3,2},{4,5},{5,4},{6,7},{7,6},{8,9},{9,8},{10,11... | collective-permute-start | bytes 3145736 | tf_op jit(solution)/shard_map/cond/branch_1_fun/ppermute | solution.py:328
  23.1 5.7 %collective-permute-start.38 = (bf16[2,128,512]{2,1,0:T(8,128)(2,1)S(1)}, bf16[2,128,512]{2,1,0:T(8,128)(2,1)S(1)}, u32[]{:S(2)}, u32[]{:S(2)}) collective-permute-start(bf16[2,128,512]{2,1,0:T(8,128)(2,1)S(1)} %branch_1_fun.8.refs_0_), channel_id=1, source_target_pairs={{0,1},{1,0},{2,3},{3,2},{4,5},{5,4},{6,7},{7,6},{8,9},{9,8},{10,11... | collective-permute-start | bytes 786440 | tf_op jit(solution)/shard_map/cond/branch_1_fun/ppermute | solution.py:328
  23.6 5.2 %collective-permute-start.39 = (bf16[2,128,512]{2,1,0:T(8,128)(2,1)S(1)}, bf16[2,128,512]{2,1,0:T(8,128)(2,1)S(1)}, u32[]{:S(2)}, u32[]{:S(2)}) collective-permute-start(bf16[2,128,512]{2,1,0:T(8,128)(2,1)S(1)} %branch_1_fun.9.refs_1_), channel_id=1, source_target_pairs={{0,1},{1,0},{2,3},{3,2},{4,5},{5,4},{6,7},{7,6},{8,9},{9,8},{10,11... | collective-permute-start | bytes 786440 | tf_op jit(solution)/shard_map/cond/branch_1_fun/ppermute | solution.py:328
  23.6 5.1 %collective-permute-start.40 = (bf16[2,128,512]{2,1,0:T(8,128)(2,1)S(1)}, bf16[2,128,512]{2,1,0:T(8,128)(2,1)S(1)}, u32[]{:S(2)}, u32[]{:S(2)}) collective-permute-start(bf16[2,128,512]{2,1,0:T(8,128)(2,1)S(1)} %collective-permute-done.36.refs_2_), channel_id=1, source_target_pairs={{0,1},{1,0},{2,3},{3,2},{4,5},{5,4},{6,7},{7,6},{8,9},{9,8},{10,11... | collective-permute-start | bytes 786440 | tf_op jit(solution)/shard_map/cond/branch_1_fun/ppermute | solution.py:328
  28.8 1.5 %collective-permute-start.41 = (bf16[2,128,512]{2,1,0:T(8,128)(2,1)S(1)}, bf16[2,128,512]{2,1,0:T(8,128)(2,1)S(1)}, u32[]{:S(2)}, u32[]{:S(2)}) collective-permute-start(bf16[2,128,512]{2,1,0:T(8,128)(2,1)S(1)} %collective-permute-done.37.refs_3_), channel_id=1, source_target_pairs={{0,1},{1,0},{2,3},{3,2},{4,5},{5,4},{6,7},{7,6},{8,9},{9,8},{10,11... | collective-permute-start | bytes 786440 | tf_op jit(solution)/shard_map/cond/branch_1_fun/ppermute | solution.py:328
  31.6 14.9 %collective-permute-start.45 = (bf16[2,128,512]{2,1,0:T(8,128)(2,1)S(1)}, bf16[2,128,512]{2,1,0:T(8,128)(2,1)S(1)}, u32[]{:S(2)}, u32[]{:S(2)}) collective-permute-start(bf16[2,128,512]{2,1,0:T(8,128)(2,1)S(1)} %get-tuple-element.44), channel_id=1, source_target_pairs={{0,8},{2,10},{4,12},{6,14},{8,0},{10,2},{12,4},{14,6},{1,9},{3,11}... | collective-permute-start | bytes 786440 | tf_op jit(solution)/shard_map/cond/branch_1_fun/ppermute | solution.py:328
  34.3 22.5 %collective-permute-start.43 = (bf16[2,2,128,512]{3,2,1,0:T(8,128)(2,1)S(1)}, bf16[2,2,128,512]{3,2,1,0:T(8,128)(2,1)S(1)}, u32[]{:S(2)}, u32[]{:S(2)}) collective-permute-start(bf16[2,2,128,512]{3,2,1,0:T(8,128)(2,1)S(1)} %get-tuple-element.43.refs_0_), channel_id=1, source_target_pairs={{0,2},{2,0},{4,6},{6,4},{8,10},{10,8},{12,14},{14,12},{1,3},{3,1},... | collective-permute-start | bytes 1572872 | tf_op jit(solution)/shard_map/cond/branch_1_fun/ppermute | solution.py:328
  46.5 10.2 %collective-permute-start.51 = (bf16[2,128,512]{2,1,0:T(8,128)(2,1)S(1)}, bf16[2,128,512]{2,1,0:T(8,128)(2,1)S(1)}, u32[]{:S(2)}, u32[]{:S(2)}) collective-permute-start(bf16[2,128,512]{2,1,0:T(8,128)(2,1)S(1)} %collective-permute-done.45.refs_4_), channel_id=1, source_target_pairs={{0,6},{2,4},{4,2},{6,0},{8,14},{10,12},{12,10},{14,8},{1,7},{3,5},... | collective-permute-start | bytes 786440 | tf_op jit(solution)/shard_map/cond/branch_1_fun/ppermute | solution.py:328
  47.9 13.3 %collective-permute-start.42 = (bf16[2,2,128,512]{3,2,1,0:T(8,128)(2,1)S(1)}, bf16[2,2,128,512]{3,2,1,0:T(8,128)(2,1)S(1)}, u32[]{:S(2)}, u32[]{:S(2)}) collective-permute-start(bf16[2,2,128,512]{3,2,1,0:T(8,128)(2,1)S(1)} %get-tuple-element.43.refs_0_), channel_id=1, source_target_pairs={{0,1},{1,0},{2,3},{3,2},{4,5},{5,4},{6,7},{7,6},{8,9},{9,8},{10,11... | collective-permute-start | bytes 1572872 | tf_op jit(solution)/shard_map/cond/branch_1_fun/ppermute | solution.py:328
  47.9 12.7 %collective-permute-start.49 = (bf16[2,128,512]{2,1,0:T(8,128)(2,1)S(1)}, bf16[2,128,512]{2,1,0:T(8,128)(2,1)S(1)}, u32[]{:S(2)}, u32[]{:S(2)}) collective-permute-start(bf16[2,128,512]{2,1,0:T(8,128)(2,1)S(1)} %collective-permute-done.45.refs_4_), channel_id=1, source_target_pairs={{0,2},{2,0},{4,6},{6,4},{8,10},{10,8},{12,14},{14,12},{1,3},{3,1},... | collective-permute-start | bytes 786440 | tf_op jit(solution)/shard_map/cond/branch_1_fun/ppermute | solution.py:328
  48.7 14.2 %copy-start.5 = (bf16[2,512,512]{2,1,0:T(8,128)(2,1)}, bf16[2,512,512]{2,1,0:T(8,128)(2,1)S(1)}, u32[]{:S(2)}) copy-start(bf16[2,512,512]{2,1,0:T(8,128)(2,1)S(1)} %collective-permute-done.33.sib_hbm) | copy-start | bytes 3145732 | tf_op jit(solution)/shard_map/cond
  48.7 11.9 %collective-permute-start.47 = (bf16[2,128,512]{2,1,0:T(8,128)(2,1)S(1)}, bf16[2,128,512]{2,1,0:T(8,128)(2,1)S(1)}, u32[]{:S(2)}, u32[]{:S(2)}) collective-permute-start(bf16[2,128,512]{2,1,0:T(8,128)(2,1)S(1)} %collective-permute-done.45.refs_4_), channel_id=1, source_target_pairs={{0,4},{2,6},{4,0},{6,2},{8,12},{10,14},{12,8},{14,10},{1,5},{3,7},... | collective-permute-start | bytes 786440 | tf_op jit(solution)/shard_map/cond/branch_1_fun/ppermute | solution.py:328
  56.7 4.4 %collective-permute-start.46 = (bf16[2,128,512]{2,1,0:T(8,128)(2,1)S(1)}, bf16[2,128,512]{2,1,0:T(8,128)(2,1)S(1)}, u32[]{:S(2)}, u32[]{:S(2)}) collective-permute-start(bf16[2,128,512]{2,1,0:T(8,128)(2,1)S(1)} %collective-permute-done.45.refs_4_), channel_id=1, source_target_pairs={{0,1},{1,0},{2,3},{3,2},{4,5},{5,4},{6,7},{7,6},{8,9},{9,8},{10,11... | collective-permute-start | bytes 786440 | tf_op jit(solution)/shard_map/cond/branch_1_fun/ppermute | solution.py:328
  56.7 6.1 %collective-permute-start.44 = (bf16[2,2,128,512]{3,2,1,0:T(8,128)(2,1)S(1)}, bf16[2,2,128,512]{3,2,1,0:T(8,128)(2,1)S(1)}, u32[]{:S(2)}, u32[]{:S(2)}) collective-permute-start(bf16[2,2,128,512]{3,2,1,0:T(8,128)(2,1)S(1)} %collective-permute-done.43.refs_2_), channel_id=1, source_target_pairs={{0,1},{1,0},{2,3},{3,2},{4,5},{5,4},{6,7},{7,6},{8,9},{9,8},{10,11... | collective-permute-start | bytes 1572872 | tf_op jit(solution)/shard_map/cond/branch_1_fun/ppermute | solution.py:328
  60.6 1.5 %collective-permute-start.52 = (bf16[2,128,512]{2,1,0:T(8,128)(2,1)S(1)}, bf16[2,128,512]{2,1,0:T(8,128)(2,1)S(1)}, u32[]{:S(2)}, u32[]{:S(2)}) collective-permute-start(bf16[2,128,512]{2,1,0:T(8,128)(2,1)S(1)} %collective-permute-done.51.refs_10_), channel_id=1, source_target_pairs={{0,1},{1,0},{2,3},{3,2},{4,5},{5,4},{6,7},{7,6},{8,9},{9,8},{10,11... | collective-permute-start | bytes 786440 | tf_op jit(solution)/shard_map/cond/branch_1_fun/ppermute | solution.py:328
  60.6 1.8 %collective-permute-start.50 = (bf16[2,128,512]{2,1,0:T(8,128)(2,1)S(1)}, bf16[2,128,512]{2,1,0:T(8,128)(2,1)S(1)}, u32[]{:S(2)}, u32[]{:S(2)}) collective-permute-start(bf16[2,128,512]{2,1,0:T(8,128)(2,1)S(1)} %collective-permute-done.49.refs_8_), channel_id=1, source_target_pairs={{0,1},{1,0},{2,3},{3,2},{4,5},{5,4},{6,7},{7,6},{8,9},{9,8},{10,11... | collective-permute-start | bytes 786440 | tf_op jit(solution)/shard_map/cond/branch_1_fun/ppermute | solution.py:328
  61.1 1.8 %collective-permute-start.48 = (bf16[2,128,512]{2,1,0:T(8,128)(2,1)S(1)}, bf16[2,128,512]{2,1,0:T(8,128)(2,1)S(1)}, u32[]{:S(2)}, u32[]{:S(2)}) collective-permute-start(bf16[2,128,512]{2,1,0:T(8,128)(2,1)S(1)} %collective-permute-done.47.refs_6_), channel_id=1, source_target_pairs={{0,1},{1,0},{2,3},{3,2},{4,5},{5,4},{6,7},{7,6},{8,9},{9,8},{10,11... | collective-permute-start | bytes 786440 | tf_op jit(solution)/shard_map/cond/branch_1_fun/ppermute | solution.py:328
  (1 other events, 1.3 us)
where the time goes:
time: 72 us; the launch traced here: 71.8 us
  waiting for transfers between devices  36.3 us (50%)
  starting transfers between devices  16.7 us (23%)
  Pallas kernels  15 us (21%)
  other arithmetic  1.43 us (2%)
  local copies, waits for them, and re-layouts  1.34 us (2%)
    ppermute x20, waiting for transfers between devices, swap(): return lax.ppermute(value, axis, [(i, i ^ bit) for i in range(n)])  36.3 us
    ppermute x20, starting transfers between devices, swap(): return lax.ppermute(value, axis, [(i, i ^ bit) for i in range(n)])  16.7 us
    pallas_call x1, Pallas kernels, stem_call(): pl.pallas_call(functools.partial(stem_kernel, plans, turn, tuple(layout))...  7.61 us
    pallas_call x2, Pallas kernels, leaf_call(): pl.pallas_call(functools.partial(kernel, plan), grid_spec=pltpu.PrefetchS...  5.25 us
    pallas_call x3, Pallas kernels, call(): pl.pallas_call(kernel, grid=(1,), in_specs=[whole(a.shape) for a in array...  2.18 us
  transfers between devices with their start and end apart: 20, of which 10 were waited for; matrix products, arithmetic and copies ran while one was open for 0% of the time, Pallas kernels for 7%

commit v1 on v0

--- a/solution.py
+++ b/solution.py
@@ -241,20 +241,25 @@
             for h, offset in halves:
                 source = ref if len(halves) == 1 else ref.at[h]
                 count = source.shape[1]
-                for s in range(2):
-                    row = jnp.where(column == 1, side, s) * half + offset
-                    row = row + (1 - zb if h else zb) * part
-                    col = jnp.where(column == 1, s, side) * half
+                at = offset + (1 - zb if h else zb) * part
+
+                @pl.when(column == 1)
+                def _():
+                    row = pl.ds(pl.multiple_of(side * half + at, count), count)
                     pltpu.make_async_copy(
-                        source.at[:, :, s * half : (s + 1) * half],
-                        o_ref.at[
-                            step,
-                            :,
-                            pl.ds(pl.multiple_of(row, count), count),
-                            pl.ds(pl.multiple_of(col, half), half),
-                        ],
-                        sem.at[step],
+                        source, o_ref.at[step, :, row], sem.at[step]
                     ).start()
+
+                @pl.when(column == 0)
+                def _():
+                    col = pl.ds(pl.multiple_of(side * half, half), half)
+                    for s in range(2):
+                        row = pl.ds(pl.multiple_of(s * half + at, count), count)
+                        pltpu.make_async_copy(
+                            source.at[:, :, s * half : (s + 1) * half],
+                            o_ref.at[step, :, row, col],
+                            sem.at[step],
+                        ).start()
 
     def arrived(step):
         pltpu.make_async_copy(o_ref.at[step], o_ref.at[step], sem.at[step]).wait()

time: 72 us -> 99.5 us (1.38)
  starting transfers between devices: 16.7 us -> 26.5 us
  waiting for transfers between devices: 36.3 us -> 45.3 us
  Pallas kernels: 15 us -> 23.6 us
    ppermute x20 -> x33, starting transfers between devices: 16.7 us -> 26.5 us  [swap(): return lax.ppermute(value, axis, [(i, i ^ bit) for i in range(n)])]
    ppermute x20 -> x33, waiting for transfers between devices: 36.3 us -> 45.3 us  [swap(): return lax.ppermute(value, axis, [(i, i ^ bit) for i in range(n)])]
    pallas_call x2 -> x4, Pallas kernels: 5.25 us -> 9.05 us  [leaf_call(): pl.pallas_call(functools.partial(kernel, plan), grid_spec=pltpu.PrefetchS...]
    pallas_call x3 -> x6, Pallas kernels: 2.18 us -> 5.75 us  [call(): pl.pallas_call(kernel, grid=(1,), in_specs=[whole(a.shape) for a in array...]
    pallas_call x0 -> x2, Pallas kernels: none -> 1.15 us  [select_call(): pl.pallas_call(functools.partial(select_kernel, plan), grid_spec=pltpu.Pr...]
  transfers between devices with their start and end apart: 20 -> 33, of which waited for: 10 -> 14; matrix products, arithmetic and copies ran while one was open for 0% -> 0% of each run, Pallas kernels for 7% -> 13%
where the time goes in v1:
time: 99.5 us; the launch traced here: 99.3 us
  waiting for transfers between devices  45.3 us (46%)
  starting transfers between devices  26.5 us (27%)
  Pallas kernels  23.6 us (24%)
  other arithmetic  1.43 us (1%)
  local copies, waits for them, and re-layouts  1.35 us (1%)
    ppermute x33, waiting for transfers between devices, swap(): return lax.ppermute(value, axis, [(i, i ^ bit) for i in range(n)])  45.3 us
    ppermute x33, starting transfers between devices, swap(): return lax.ppermute(value, axis, [(i, i ^ bit) for i in range(n)])  26.5 us
    pallas_call x4, Pallas kernels, leaf_call(): pl.pallas_call(functools.partial(kernel, plan), grid_spec=pltpu.PrefetchS...  9.05 us
    pallas_call x1, Pallas kernels, stem_call(): pl.pallas_call(functools.partial(stem_kernel, plans, turn, tuple(layout))...  7.62 us
    pallas_call x6, Pallas kernels, call(): pl.pallas_call(kernel, grid=(1,), in_specs=[whole(a.shape) for a in array...  5.75 us
  transfers between devices with their start and end apart: 33, of which 14 were waited for; matrix products, arithmetic and copies ran while one was open for 0% of the time, Pallas kernels for 13%

profile of v1, /device:TPU:0, one launch (start us, length us, event | category | flops | bytes accessed | tf_op | source)
XLA Modules:
  0.0 99.3 jit_solution(14327236214691496870)
XLA Ops:
  2.0 96.0 %conditional.1 = (f32[2,512,512]{2,1,0:T(8,128)S(1)}) conditional(s32[]{:T(128)} %convert_element_type.9, (f32[2,512,512]{2,1,0:T(8,128)}, s32[4]{0:T(128)}, s32[4,9]{1,0:T(4,128)}, bf16[1,4,2,512,512]{4,3,2,1,0:T(8,128)(2,1)}) %tuple.14, (f32[2,512,512]{2,1,0:T(8,128)}, s32[4]{0:T(128)}, s32[4,9]{1,0:T(4,128)}, ...), branch_computations={%region_1.2_spmd, %region_2.3_spmd} | conditional | flops 524288 | bytes 72353904 | solution.py:483
  2.0 2.7 %branch_0_fun.13 = (bf16[2,128,512]{2,1,0:T(8,128)(2,1)}, bf16[2,128,512]{2,1,0:T(8,128)(2,1)}) custom-call(s32[4]{0:T(128)} %get-tuple-element.24.roots_ref, s32[4,9]{1,0:T(4,128)} %get-tuple-element.26.modes_ref, bf16[1,4,2,512,512]{4,3,2,1,0:T(8,128)(2,1)} %get-tuple-element.30.leaves_ref), custom_call_target="tpu_custom_call" | custom-call | tf_op jit(solution)/shard_map/cond/branch_0_fun/pallas_call | solution.py:122
  4.7 3.7 %collective-permute-start.1 = (bf16[2,128,512]{2,1,0:T(8,128)(2,1)}, bf16[2,128,512]{2,1,0:T(8,128)(2,1)S(1)}, u32[]{:S(2)}, u32[]{:S(2)}) collective-permute-start(bf16[2,128,512]{2,1,0:T(8,128)(2,1)} %get-tuple-element.28), channel_id=1, source_target_pairs={{0,2},{2,0},{4,6},{6,4},{8,10},{10,8},{12,14},{14,12},{1,3},{3,1},... | collective-permute-start | bytes 786440 | tf_op jit(solution)/shard_map/cond/branch_0_fun/ppermute | solution.py:333
  8.5 2.4 %branch_0_fun.14 = (bf16[2,128,512]{2,1,0:T(8,128)(2,1)}, bf16[2,128,512]{2,1,0:T(8,128)(2,1)}) custom-call(s32[4]{0:T(128)S(1)} %copy-done.8, s32[4,9]{1,0:T(4,128)S(1)} %copy-done.6, bf16[1,4,2,512,512]{4,3,2,1,0:T(8,128)(2,1)} %get-tuple-element.30.leaves_ref), custom_call_target="tpu_custom_call" | custom-call | tf_op jit(solution)/shard_map/cond/branch_0_fun/pallas_call | solution.py:122
  10.9 2.6 %branch_0_fun.15.right_ref = bf16[2,512,512]{2,1,0:T(8,128)(2,1)S(1)} custom-call(s32[4]{0:T(128)S(1)} %copy-done.8, s32[4,9]{1,0:T(4,128)S(1)} %copy-done.6, bf16[1,4,2,512,512]{4,3,2,1,0:T(8,128)(2,1)} %get-tuple-element.30.leaves_ref), custom_call_target="tpu_custom_call" | custom-call | tf_op jit(solution)/shard_map/cond/branch_0_fun/pallas_call | solution.py:122
  13.5 2.2 %collective-permute-done.1.left_ref = bf16[2,128,512]{2,1,0:T(8,128)(2,1)S(1)} collective-permute-done((bf16[2,128,512]{2,1,0:T(8,128)(2,1)}, bf16[2,128,512]{2,1,0:T(8,128)(2,1)S(1)}, u32[]{:S(2)}, u32[]{:S(2)}) %collective-permute-start.1) | collective-permute-done | bytes 262176 | tf_op jit(solution)/shard_map/cond/branch_0_fun/ppermute | solution.py:333
  16.2 1.6 %collective-permute-start.3 = (bf16[2,128,512]{2,1,0:T(8,128)(2,1)S(1)}, bf16[2,128,512]{2,1,0:T(8,128)(2,1)S(1)}, u32[]{:S(2)}, u32[]{:S(2)}) collective-permute-start(bf16[2,128,512]{2,1,0:T(8,128)(2,1)S(1)} %branch_0_fun.16.refs_0_), channel_id=1, source_target_pairs={{0,4},{2,6},{4,0},{6,2},{8,12},{10,14},{12,8},{14,10},{1,5},{3,7},... | collective-permute-start | bytes 786440 | tf_op jit(solution)/shard_map/cond/branch_0_fun/ppermute | solution.py:333
  17.8 2.7 %collective-permute-done.2.left_ref = bf16[2,128,512]{2,1,0:T(8,128)(2,1)S(1)} collective-permute-done((bf16[2,128,512]{2,1,0:T(8,128)(2,1)}, bf16[2,128,512]{2,1,0:T(8,128)(2,1)S(1)}, u32[]{:S(2)}, u32[]{:S(2)}) %collective-permute-start.2) | collective-permute-done | bytes 262176 | tf_op jit(solution)/shard_map/cond/branch_0_fun/ppermute | solution.py:333
  21.0 1.6 %collective-permute-start.4 = (bf16[2,128,512]{2,1,0:T(8,128)(2,1)S(1)}, bf16[2,128,512]{2,1,0:T(8,128)(2,1)S(1)}, u32[]{:S(2)}, u32[]{:S(2)}) collective-permute-start(bf16[2,128,512]{2,1,0:T(8,128)(2,1)S(1)} %branch_0_fun.17.refs_1_), channel_id=1, source_target_pairs={{0,4},{2,6},{4,0},{6,2},{8,12},{10,14},{12,8},{14,10},{1,5},{3,7},... | collective-permute-start | bytes 786440 | tf_op jit(solution)/shard_map/cond/branch_0_fun/ppermute | solution.py:333
  22.6 1.7 %collective-permute-start.17 = (bf16[2,128,512]{2,1,0:T(8,128)(2,1)S(1)}, bf16[2,128,512]{2,1,0:T(8,128)(2,1)S(1)}, u32[]{:S(2)}, u32[]{:S(2)}) collective-permute-start(bf16[2,128,512]{2,1,0:T(8,128)(2,1)S(1)} %copy-done.11), channel_id=1, source_target_pairs={{0,2},{2,0},{4,6},{6,4},{8,10},{10,8},{12,14},{14,12},{1,3},{3,1},... | collective-permute-start | bytes 786440 | tf_op jit(solution)/shard_map/cond/branch_0_fun/ppermute | solution.py:333
  24.9 3.7 %collective-permute-done.4.refs_3_ = bf16[2,128,512]{2,1,0:T(8,128)(2,1)S(1)} collective-permute-done((bf16[2,128,512]{2,1,0:T(8,128)(2,1)S(1)}, bf16[2,128,512]{2,1,0:T(8,128)(2,1)S(1)}, u32[]{:S(2)}, u32[]{:S(2)}) %collective-permute-start.4) | collective-permute-done | bytes 262176 | tf_op jit(solution)/shard_map/cond/branch_0_fun/ppermute | solution.py:333
  34.3 2.0 %branch_0_fun.18 = (bf16[2,128,512]{2,1,0:T(8,128)(2,1)S(1)}, bf16[2,128,512]{2,1,0:T(8,128)(2,1)}) custom-call(bf16[2,128,512]{2,1,0:T(8,128)(2,1)S(1)} %branch_0_fun.16.refs_0_, bf16[2,128,512]{2,1,0:T(8,128)(2,1)S(1)} %branch_0_fun.17.refs_1_, bf16[2,128,512]{2,1,0:T(8,128)(2,1)S(1)} %collective-permute-done.3.refs_2_, ...), custom_call_target="tpu_custom_call" | custom-call | tf_op jit(solution)/shard_map/cond/branch_0_fun/pallas_call | solution.py:141
  36.3 2.6 %collective-permute-start.9 = (bf16[2,128,512]{2,1,0:T(8,128)(2,1)S(1)}, bf16[2,128,512]{2,1,0:T(8,128)(2,1)S(1)}, u32[]{:S(2)}, u32[]{:S(2)}) collective-permute-start(bf16[2,128,512]{2,1,0:T(8,128)(2,1)S(1)} %get-tuple-element.32.made_ref), channel_id=1, source_target_pairs={{0,8},{2,10},{4,12},{6,14},{8,0},{10,2},{12,4},{14,6},{1,9},{3,11}... | collective-permute-start | bytes 786440 | tf_op jit(solution)/shard_map/cond/branch_0_fun/ppermute | solution.py:333
  40.6 6.4 %collective-permute-done.19.refs_2_ = bf16[2,128,512]{2,1,0:T(8,128)(2,1)S(1)} collective-permute-done((bf16[2,128,512]{2,1,0:T(8,128)(2,1)S(1)}, bf16[2,128,512]{2,1,0:T(8,128)(2,1)S(1)}, u32[]{:S(2)}, u32[]{:S(2)}) %collective-permute-start.19) | collective-permute-done | bytes 262176 | tf_op jit(solution)/shard_map/cond/branch_0_fun/ppermute | solution.py:333
  46.9 4.3 %collective-permute-done.9.other_ref = bf16[2,128,512]{2,1,0:T(8,128)(2,1)S(1)} collective-permute-done((bf16[2,128,512]{2,1,0:T(8,128)(2,1)S(1)}, bf16[2,128,512]{2,1,0:T(8,128)(2,1)S(1)}, u32[]{:S(2)}, u32[]{:S(2)}) %collective-permute-start.9) | collective-permute-done | bytes 262176 | tf_op jit(solution)/shard_map/cond/branch_0_fun/ppermute | solution.py:333
  51.2 2.2 %collective-permute-done.20.refs_3_ = bf16[2,128,512]{2,1,0:T(8,128)(2,1)S(1)} collective-permute-done((bf16[2,128,512]{2,1,0:T(8,128)(2,1)S(1)}, bf16[2,128,512]{2,1,0:T(8,128)(2,1)S(1)}, u32[]{:S(2)}, u32[]{:S(2)}) %collective-permute-start.20) | collective-permute-done | bytes 262176 | tf_op jit(solution)/shard_map/cond/branch_0_fun/ppermute | solution.py:333
  56.3 2.0 %branch_0_fun.23 = (bf16[2,128,512]{2,1,0:T(8,128)(2,1)S(1)}, bf16[2,128,512]{2,1,0:T(8,128)(2,1)}) custom-call(bf16[2,128,512]{2,1,0:T(8,128)(2,1)S(1)} %branch_0_fun.21.refs_0_, bf16[2,128,512]{2,1,0:T(8,128)(2,1)S(1)} %branch_0_fun.22.refs_1_, bf16[2,128,512]{2,1,0:T(8,128)(2,1)S(1)} %collective-permute-done.19.refs_2_, ...), custom_call_target="tpu_custom_call" | custom-call | tf_op jit(solution)/shard_map/cond/branch_0_fun/pallas_call | solution.py:141
  58.2 2.5 %collective-permute-start.25 = (bf16[2,128,512]{2,1,0:T(8,128)(2,1)S(1)}, bf16[2,128,512]{2,1,0:T(8,128)(2,1)S(1)}, u32[]{:S(2)}, u32[]{:S(2)}) collective-permute-start(bf16[2,128,512]{2,1,0:T(8,128)(2,1)S(1)} %get-tuple-element.36.made_ref), channel_id=1, source_target_pairs={{0,8},{2,10},{4,12},{6,14},{8,0},{10,2},{12,4},{14,6},{1,9},{3,11}... | collective-permute-start | bytes 786440 | tf_op jit(solution)/shard_map/cond/branch_0_fun/ppermute | solution.py:333
  62.1 6.8 %collective-permute-done.15.refs_6_ = bf16[2,128,512]{2,1,0:T(8,128)(2,1)S(1)} collective-permute-done((bf16[2,128,512]{2,1,0:T(8,128)(2,1)S(1)}, bf16[2,128,512]{2,1,0:T(8,128)(2,1)S(1)}, u32[]{:S(2)}, u32[]{:S(2)}) %collective-permute-start.15) | collective-permute-done | bytes 262176 | tf_op jit(solution)/shard_map/cond/branch_0_fun/ppermute | solution.py:333
  69.4 3.7 %collective-permute-done.25.other_ref = bf16[2,128,512]{2,1,0:T(8,128)(2,1)S(1)} collective-permute-done((bf16[2,128,512]{2,1,0:T(8,128)(2,1)S(1)}, bf16[2,128,512]{2,1,0:T(8,128)(2,1)S(1)}, u32[]{:S(2)}, u32[]{:S(2)}) %collective-permute-start.25) | collective-permute-done | bytes 262176 | tf_op jit(solution)/shard_map/cond/branch_0_fun/ppermute | solution.py:333
  75.6 1.6 %collective-permute-start.27 = (bf16[2,128,512]{2,1,0:T(8,128)(2,1)S(1)}, bf16[2,128,512]{2,1,0:T(8,128)(2,1)S(1)}, u32[]{:S(2)}, u32[]{:S(2)}) collective-permute-start(bf16[2,128,512]{2,1,0:T(8,128)(2,1)S(1)} %branch_0_fun.24.refs_8_), channel_id=1, source_target_pairs={{0,4},{2,6},{4,0},{6,2},{8,12},{10,14},{12,8},{14,10},{1,5},{3,7},... | collective-permute-start | bytes 786440 | tf_op jit(solution)/shard_map/cond/branch_0_fun/ppermute | solution.py:333
  77.8 6.0 %collective-permute-done.31.refs_14_ = bf16[2,128,512]{2,1,0:T(8,128)(2,1)S(1)} collective-permute-done((bf16[2,128,512]{2,1,0:T(8,128)(2,1)S(1)}, bf16[2,128,512]{2,1,0:T(8,128)(2,1)S(1)}, u32[]{:S(2)}, u32[]{:S(2)}) %collective-permute-start.31) | collective-permute-done | bytes 262176 | tf_op jit(solution)/shard_map/cond/branch_0_fun/ppermute | solution.py:333
  83.8 4.4 %collective-permute-done.29.refs_12_ = bf16[2,128,512]{2,1,0:T(8,128)(2,1)S(1)} collective-permute-done((bf16[2,128,512]{2,1,0:T(8,128)(2,1)S(1)}, bf16[2,128,512]{2,1,0:T(8,128)(2,1)S(1)}, u32[]{:S(2)}, u32[]{:S(2)}) %collective-permute-start.29) | collective-permute-done | bytes 262176 | tf_op jit(solution)/shard_map/cond/branch_0_fun/ppermute | solution.py:333
  90.1 7.6 %branch_0_fun.25 = f32[2,512,512]{2,1,0:T(8,128)S(1)} custom-call(s32[4]{0:T(128)S(1)} %copy-done.8, bf16[2,512,512]{2,1,0:T(8,128)(2,1)S(1)} %convert_element_type.6.own_hbm, bf16[2,512,512]{2,1,0:T(8,128)(2,1)} %copy-done.4, bf16[2,128,512]{2,1,0:T(8,128)(2,1)S(1)} %branch_0_fun.19.refs_0_, bf16[2,128,512]{2,1,0:T(8,128)(2,1)S(1)} %collective-permute-done.10.refs_1_, ...), custom_call_target="tpu_custom_call" | custom-call | tf_op jit(solution)/shard_map/cond/branch_0_fun/pallas_call | solution.py:310
  (74 shorter events, 21.2 us)
Async XLA Ops:
  4.7 11.1 %collective-permute-start.1 = (bf16[2,128,512]{2,1,0:T(8,128)(2,1)}, bf16[2,128,512]{2,1,0:T(8,128)(2,1)S(1)}, u32[]{:S(2)}, u32[]{:S(2)}) collective-permute-start(bf16[2,128,512]{2,1,0:T(8,128)(2,1)} %get-tuple-element.28), channel_id=1, source_target_pairs={{0,2},{2,0},{4,6},{6,4},{8,10},{10,8},{12,14},{14,12},{1,3},{3,1},... | collective-permute-start | bytes 786440 | tf_op jit(solution)/shard_map/cond/branch_0_fun/ppermute | solution.py:333
  8.4 12.1 %collective-permute-start.2 = (bf16[2,128,512]{2,1,0:T(8,128)(2,1)}, bf16[2,128,512]{2,1,0:T(8,128)(2,1)S(1)}, u32[]{:S(2)}, u32[]{:S(2)}) collective-permute-start(bf16[2,128,512]{2,1,0:T(8,128)(2,1)} %get-tuple-element.31), channel_id=1, source_target_pairs={{0,2},{2,0},{4,6},{6,4},{8,10},{10,8},{12,14},{14,12},{1,3},{3,1},... | collective-permute-start | bytes 786440 | tf_op jit(solution)/shard_map/cond/branch_0_fun/ppermute | solution.py:333
  16.2 8.7 %collective-permute-start.3 = (bf16[2,128,512]{2,1,0:T(8,128)(2,1)S(1)}, bf16[2,128,512]{2,1,0:T(8,128)(2,1)S(1)}, u32[]{:S(2)}, u32[]{:S(2)}) collective-permute-start(bf16[2,128,512]{2,1,0:T(8,128)(2,1)S(1)} %branch_0_fun.16.refs_0_), channel_id=1, source_target_pairs={{0,4},{2,6},{4,0},{6,2},{8,12},{10,14},{12,8},{14,10},{1,5},{3,7},... | collective-permute-start | bytes 786440 | tf_op jit(solution)/shard_map/cond/branch_0_fun/ppermute | solution.py:333
  21.0 7.6 %collective-permute-start.4 = (bf16[2,128,512]{2,1,0:T(8,128)(2,1)S(1)}, bf16[2,128,512]{2,1,0:T(8,128)(2,1)S(1)}, u32[]{:S(2)}, u32[]{:S(2)}) collective-permute-start(bf16[2,128,512]{2,1,0:T(8,128)(2,1)S(1)} %branch_0_fun.17.refs_1_), channel_id=1, source_target_pairs={{0,4},{2,6},{4,0},{6,2},{8,12},{10,14},{12,8},{14,10},{1,5},{3,7},... | collective-permute-start | bytes 786440 | tf_op jit(solution)/shard_map/cond/branch_0_fun/ppermute | solution.py:333
  22.6 7.2 %collective-permute-start.17 = (bf16[2,128,512]{2,1,0:T(8,128)(2,1)S(1)}, bf16[2,128,512]{2,1,0:T(8,128)(2,1)S(1)}, u32[]{:S(2)}, u32[]{:S(2)}) collective-permute-start(bf16[2,128,512]{2,1,0:T(8,128)(2,1)S(1)} %copy-done.11), channel_id=1, source_target_pairs={{0,2},{2,0},{4,6},{6,4},{8,10},{10,8},{12,14},{14,12},{1,3},{3,1},... | collective-permute-start | bytes 786440 | tf_op jit(solution)/shard_map/cond/branch_0_fun/ppermute | solution.py:333
  24.4 9.0 %collective-permute-start.6 = (bf16[2,128,512]{2,1,0:T(8,128)(2,1)S(1)}, bf16[2,128,512]{2,1,0:T(8,128)(2,1)S(1)}, u32[]{:S(2)}, u32[]{:S(2)}) collective-permute-start(bf16[2,128,512]{2,1,0:T(8,128)(2,1)S(1)} %branch_0_fun.17.refs_1_), channel_id=1, source_target_pairs={{0,1},{1,0},{2,3},{3,2},{4,5},{5,4},{6,7},{7,6},{8,9},{9,8},{10,11... | collective-permute-start | bytes 786440 | tf_op jit(solution)/shard_map/cond/branch_0_fun/ppermute | solution.py:333
  24.9 9.4 %collective-permute-start.7 = (bf16[2,128,512]{2,1,0:T(8,128)(2,1)S(1)}, bf16[2,128,512]{2,1,0:T(8,128)(2,1)S(1)}, u32[]{:S(2)}, u32[]{:S(2)}) collective-permute-start(bf16[2,128,512]{2,1,0:T(8,128)(2,1)S(1)} %collective-permute-done.3.refs_2_), channel_id=1, source_target_pairs={{0,1},{1,0},{2,3},{3,2},{4,5},{5,4},{6,7},{7,6},{8,9},{9,8},{10,11... | collective-permute-start | bytes 786440 | tf_op jit(solution)/shard_map/cond/branch_0_fun/ppermute | solution.py:333
  29.8 9.0 %collective-permute-start.18 = (bf16[2,128,512]{2,1,0:T(8,128)(2,1)S(1)}, bf16[2,128,512]{2,1,0:T(8,128)(2,1)S(1)}, u32[]{:S(2)}, u32[]{:S(2)}) collective-permute-start(bf16[2,128,512]{2,1,0:T(8,128)(2,1)S(1)} %copy-done.10), channel_id=1, source_target_pairs={{0,2},{2,0},{4,6},{6,4},{8,10},{10,8},{12,14},{14,12},{1,3},{3,1},... | collective-permute-start | bytes 786440 | tf_op jit(solution)/shard_map/cond/branch_0_fun/ppermute | solution.py:333
  31.4 42.2 %collective-permute-start = (bf16[2,512,512]{2,1,0:T(8,128)(2,1)S(1)}, bf16[2,512,512]{2,1,0:T(8,128)(2,1)S(1)}, u32[]{:S(2)}, u32[]{:S(2)}) collective-permute-start(bf16[2,512,512]{2,1,0:T(8,128)(2,1)S(1)} %convert_element_type.6.own_hbm), channel_id=1, source_target_pairs={{0,1},{1,0},{2,3},{3,2},{4,5},{5,4},{6,7},{7,6},{8,9},{9,8},{10,11... | collective-permute-start | bytes 3145736 | tf_op jit(solution)/shard_map/cond/branch_0_fun/ppermute | solution.py:333
  33.4 13.5 %collective-permute-start.19 = (bf16[2,128,512]{2,1,0:T(8,128)(2,1)S(1)}, bf16[2,128,512]{2,1,0:T(8,128)(2,1)S(1)}, u32[]{:S(2)}, u32[]{:S(2)}) collective-permute-start(bf16[2,128,512]{2,1,0:T(8,128)(2,1)S(1)} %branch_0_fun.21.refs_0_), channel_id=1, source_target_pairs={{0,4},{2,6},{4,0},{6,2},{8,12},{10,14},{12,8},{14,10},{1,5},{3,7},... | collective-permute-start | bytes 786440 | tf_op jit(solution)/shard_map/cond/branch_0_fun/ppermute | solution.py:333
  36.3 15.0 %collective-permute-start.9 = (bf16[2,128,512]{2,1,0:T(8,128)(2,1)S(1)}, bf16[2,128,512]{2,1,0:T(8,128)(2,1)S(1)}, u32[]{:S(2)}, u32[]{:S(2)}) collective-permute-start(bf16[2,128,512]{2,1,0:T(8,128)(2,1)S(1)} %get-tuple-element.32.made_ref), channel_id=1, source_target_pairs={{0,8},{2,10},{4,12},{6,14},{8,0},{10,2},{12,4},{14,6},{1,9},{3,11}... | collective-permute-start | bytes 786440 | tf_op jit(solution)/shard_map/cond/branch_0_fun/ppermute | solution.py:333
  39.3 14.0 %collective-permute-start.20 = (bf16[2,128,512]{2,1,0:T(8,128)(2,1)S(1)}, bf16[2,128,512]{2,1,0:T(8,128)(2,1)S(1)}, u32[]{:S(2)}, u32[]{:S(2)}) collective-permute-start(bf16[2,128,512]{2,1,0:T(8,128)(2,1)S(1)} %branch_0_fun.22.refs_1_), channel_id=1, source_target_pairs={{0,4},{2,6},{4,0},{6,2},{8,12},{10,14},{12,8},{14,10},{1,5},{3,7},... | collective-permute-start | bytes 786440 | tf_op jit(solution)/shard_map/cond/branch_0_fun/ppermute | solution.py:333
  40.5 13.4 %collective-permute-start.21 = (bf16[2,128,512]{2,1,0:T(8,128)(2,1)S(1)}, bf16[2,128,512]{2,1,0:T(8,128)(2,1)S(1)}, u32[]{:S(2)}, u32[]{:S(2)}) collective-permute-start(bf16[2,128,512]{2,1,0:T(8,128)(2,1)S(1)} %branch_0_fun.21.refs_0_), channel_id=1, source_target_pairs={{0,1},{1,0},{2,3},{3,2},{4,5},{5,4},{6,7},{7,6},{8,9},{9,8},{10,11... | collective-permute-start | bytes 786440 | tf_op jit(solution)/shard_map/cond/branch_0_fun/ppermute | solution.py:333
  46.9 7.7 %collective-permute-start.22 = (bf16[2,128,512]{2,1,0:T(8,128)(2,1)S(1)}, bf16[2,128,512]{2,1,0:T(8,128)(2,1)S(1)}, u32[]{:S(2)}, u32[]{:S(2)}) collective-permute-start(bf16[2,128,512]{2,1,0:T(8,128)(2,1)S(1)} %branch_0_fun.22.refs_1_), channel_id=1, source_target_pairs={{0,1},{1,0},{2,3},{3,2},{4,5},{5,4},{6,7},{7,6},{8,9},{9,8},{10,11... | collective-permute-start | bytes 786440 | tf_op jit(solution)/shard_map/cond/branch_0_fun/ppermute | solution.py:333
  54.0 14.9 %collective-permute-start.15 = (bf16[2,128,512]{2,1,0:T(8,128)(2,1)S(1)}, bf16[2,128,512]{2,1,0:T(8,128)(2,1)S(1)}, u32[]{:S(2)}, u32[]{:S(2)}) collective-permute-start(bf16[2,128,512]{2,1,0:T(8,128)(2,1)S(1)} %branch_0_fun.19.refs_0_), channel_id=1, source_target_pairs={{0,6},{2,4},{4,2},{6,0},{8,14},{10,12},{12,10},{14,8},{1,7},{3,5},... | collective-permute-start | bytes 786440 | tf_op jit(solution)/shard_map/cond/branch_0_fun/ppermute | solution.py:333
  54.6 14.3 %collective-permute-start.13 = (bf16[2,128,512]{2,1,0:T(8,128)(2,1)S(1)}, bf16[2,128,512]{2,1,0:T(8,128)(2,1)S(1)}, u32[]{:S(2)}, u32[]{:S(2)}) collective-permute-start(bf16[2,128,512]{2,1,0:T(8,128)(2,1)S(1)} %branch_0_fun.19.refs_0_), channel_id=1, source_target_pairs={{0,2},{2,0},{4,6},{6,4},{8,10},{10,8},{12,14},{14,12},{1,3},{3,1},... | collective-permute-start | bytes 786440 | tf_op jit(solution)/shard_map/cond/branch_0_fun/ppermute | solution.py:333
  58.2 14.8 %collective-permute-start.25 = (bf16[2,128,512]{2,1,0:T(8,128)(2,1)S(1)}, bf16[2,128,512]{2,1,0:T(8,128)(2,1)S(1)}, u32[]{:S(2)}, u32[]{:S(2)}) collective-permute-start(bf16[2,128,512]{2,1,0:T(8,128)(2,1)S(1)} %get-tuple-element.36.made_ref), channel_id=1, source_target_pairs={{0,8},{2,10},{4,12},{6,14},{8,0},{10,2},{12,4},{14,6},{1,9},{3,11}... | collective-permute-start | bytes 786440 | tf_op jit(solution)/shard_map/cond/branch_0_fun/ppermute | solution.py:333
  60.8 13.3 %collective-permute-start.11 = (bf16[2,128,512]{2,1,0:T(8,128)(2,1)S(1)}, bf16[2,128,512]{2,1,0:T(8,128)(2,1)S(1)}, u32[]{:S(2)}, u32[]{:S(2)}) collective-permute-start(bf16[2,128,512]{2,1,0:T(8,128)(2,1)S(1)} %branch_0_fun.19.refs_0_), channel_id=1, source_target_pairs={{0,4},{2,6},{4,0},{6,2},{8,12},{10,14},{12,8},{14,10},{1,5},{3,7},... | collective-permute-start | bytes 786440 | tf_op jit(solution)/shard_map/cond/branch_0_fun/ppermute | solution.py:333
  68.9 8.4 %collective-permute-start.16 = (bf16[2,128,512]{2,1,0:T(8,128)(2,1)S(1)}, bf16[2,128,512]{2,1,0:T(8,128)(2,1)S(1)}, u32[]{:S(2)}, u32[]{:S(2)}) collective-permute-start(bf16[2,128,512]{2,1,0:T(8,128)(2,1)S(1)} %collective-permute-done.15.refs_6_), channel_id=1, source_target_pairs={{0,1},{1,0},{2,3},{3,2},{4,5},{5,4},{6,7},{7,6},{8,9},{9,8},{10,11... | collective-permute-start | bytes 786440 | tf_op jit(solution)/shard_map/cond/branch_0_fun/ppermute | solution.py:333
  73.7 10.1 %collective-permute-start.31 = (bf16[2,128,512]{2,1,0:T(8,128)(2,1)S(1)}, bf16[2,128,512]{2,1,0:T(8,128)(2,1)S(1)}, u32[]{:S(2)}, u32[]{:S(2)}) collective-permute-start(bf16[2,128,512]{2,1,0:T(8,128)(2,1)S(1)} %branch_0_fun.24.refs_8_), channel_id=1, source_target_pairs={{0,6},{2,4},{4,2},{6,0},{8,14},{10,12},{12,10},{14,8},{1,7},{3,5},... | collective-permute-start | bytes 786440 | tf_op jit(solution)/shard_map/cond/branch_0_fun/ppermute | solution.py:333
  74.1 14.1 %collective-permute-start.29 = (bf16[2,128,512]{2,1,0:T(8,128)(2,1)S(1)}, bf16[2,128,512]{2,1,0:T(8,128)(2,1)S(1)}, u32[]{:S(2)}, u32[]{:S(2)}) collective-permute-start(bf16[2,128,512]{2,1,0:T(8,128)(2,1)S(1)} %branch_0_fun.24.refs_8_), channel_id=1, source_target_pairs={{0,2},{2,0},{4,6},{6,4},{8,10},{10,8},{12,14},{14,12},{1,3},{3,1},... | collective-permute-start | bytes 786440 | tf_op jit(solution)/shard_map/cond/branch_0_fun/ppermute | solution.py:333
  75.6 12.6 %collective-permute-start.27 = (bf16[2,128,512]{2,1,0:T(8,128)(2,1)S(1)}, bf16[2,128,512]{2,1,0:T(8,128)(2,1)S(1)}, u32[]{:S(2)}, u32[]{:S(2)}) collective-permute-start(bf16[2,128,512]{2,1,0:T(8,128)(2,1)S(1)} %branch_0_fun.24.refs_8_), channel_id=1, source_target_pairs={{0,4},{2,6},{4,0},{6,2},{8,12},{10,14},{12,8},{14,10},{1,5},{3,7},... | collective-permute-start | bytes 786440 | tf_op jit(solution)/shard_map/cond/branch_0_fun/ppermute | solution.py:333
  77.2 11.4 %collective-permute-start.12 = (bf16[2,128,512]{2,1,0:T(8,128)(2,1)S(1)}, bf16[2,128,512]{2,1,0:T(8,128)(2,1)S(1)}, u32[]{:S(2)}, u32[]{:S(2)}) collective-permute-start(bf16[2,128,512]{2,1,0:T(8,128)(2,1)S(1)} %collective-permute-done.11.refs_2_), channel_id=1, source_target_pairs={{0,1},{1,0},{2,3},{3,2},{4,5},{5,4},{6,7},{7,6},{8,9},{9,8},{10,11... | collective-permute-start | bytes 786440 | tf_op jit(solution)/shard_map/cond/branch_0_fun/ppermute | solution.py:333
  77.3 11.4 %collective-permute-start.26 = (bf16[2,128,512]{2,1,0:T(8,128)(2,1)S(1)}, bf16[2,128,512]{2,1,0:T(8,128)(2,1)S(1)}, u32[]{:S(2)}, u32[]{:S(2)}) collective-permute-start(bf16[2,128,512]{2,1,0:T(8,128)(2,1)S(1)} %branch_0_fun.24.refs_8_), channel_id=1, source_target_pairs={{0,1},{1,0},{2,3},{3,2},{4,5},{5,4},{6,7},{7,6},{8,9},{9,8},{10,11... | collective-permute-start | bytes 786440 | tf_op jit(solution)/shard_map/cond/branch_0_fun/ppermute | solution.py:333
  (17 other events, 134.4 us)
